TPU v7x, 256 devices: a whole 4x4x8 slice. The times are simulated.
256 devices in a mesh: outer: 8 (over z), inner: 32 (over x, y, core).
Axes of the slice: x: 4, y: 4, z: 8, core: 2. Of those that a mesh axis runs over, the one named last changes fastest.
Arguments:
- b_leaf: float32 [65536, 64], P(('outer', 'inner')), may hold values from -6 to 6
- b_sep: float32 [2048, 64], P(('outer', 'inner')), may hold values from -6 to 6
- b_root: float32 [2048, 64], P(('outer', 'inner')), may hold values from -6 to 6
- leaf_linv: float32 [65536, 256], P(('outer', 'inner')), as said below
- leaf_uinv: float32 [65536, 256], P(('outer', 'inner')), as said below
- leaf_lower: float32 [65536, 256], P(('outer', 'inner')), as said below
- leaf_upper: float32 [65536, 256], P(('outer', 'inner')), as said below
- sep_rows: int32 [256, 256], P(('outer', 'inner')), may hold values from 0 to 255, as said below
- sep_linv: float32 [2048, 256], P(('outer', 'inner')), as said below
- sep_uinv: float32 [2048, 256], P(('outer', 'inner')), as said below
- sep_lower: float32 [2048, 2048], P(None, ('outer', 'inner')), as said below
- sep_upper: float32 [2048, 2048], P(('outer', 'inner')), as said below
- root_linv: float32 [2048, 2048], P(('outer', 'inner')), as said below
- root_uinv: float32 [2048, 2048], P(('outer', 'inner')), as said below
- basis_leaf: float32 [65536, 512], P(('outer', 'inner')), as said below
- basis_sep: float32 [2048, 512], P(('outer', 'inner')), as said below
- basis_root: float32 [2048, 512], P(('outer', 'inner')), as said below
- g_blocks: float32 [262144, 128], P(('outer', 'inner')), may hold values from -0.25 to 0.25
- c_blocks: float32 [262144, 128], P(('outer', 'inner')), may hold values from -0.25 to 0.25
- block_cols: int32 [512, 4], P(('outer', 'inner')), may hold values from 0 to 1
Outputs:
- v_leaf: float32 [65536, 64], P(('outer', 'inner'))
- v_sep: float32 [2048, 64], P(('outer', 'inner'))
- v_root: float32 [2048, 64], P(('outer', 'inner'))
- coefficients: float32 [512, 64], replicated
- reduced_g: float32 [64, 64], replicated
- reduced_c: float32 [64, 64], replicated
Inputs may be any that keep to these rules, and one draw needn't show every extreme that they name: `sep_rows`: each row holds 256 distinct numbers; every row names 0 and 255. `leaf_linv`: lower triangular in each diagonal block of the stack, nonzero diagonal. `leaf_uinv`: upper triangular in each diagonal block of the stack, nonzero diagonal. `sep_linv`: lower triangular in each block of 256 rows, nonzero diagonal. `sep_uinv`: upper triangular in each block of 256 rows, nonzero diagonal. `root_linv`: lower triangular, nonzero diagonal. `root_uinv`: upper triangular, nonzero diagonal. `leaf_lower`: entries of order one over the square root of 256. `leaf_upper`: entries of order one over the square root of 256. `sep_lower`: entries of order one over the square root of the number of its columns. `sep_upper`: entries of order one over the square root of 2048. basis_leaf, basis_sep and basis_root stacked by rows form Q with Q^T Q = 69632 I up to float32 rounding. `basis_sep`: part of the stacked Q described with basis_leaf. `basis_root`: part of the stacked Q described with basis_leaf.
All inputs are finite; a program needn't handle non-finite values.
Results may differ from a plain program's by a relative error of at most 0.0003.
Values sent between devices are 32-bit elements; how exact they have to be, the bound alone decides.
A program may use at most 64 MiB of HBM per device.

v0:
```python
import jax
import jax.numpy as jnp
from jax import lax
from jax.sharding import PartitionSpec as P


def matmul_exact(left, right):
    return jnp.dot(left, right, precision=lax.Precision.HIGHEST, preferred_element_type=jnp.float32)


def contract_rows(left, right):
    return lax.dot_general(
        left,
        right,
        (((0,), (0,)), ((), ())),
        precision=lax.Precision.HIGHEST,
        preferred_element_type=jnp.float32,
    )


def shards(
    b_leaf,
    b_sep,
    b_root,
    leaf_linv,
    leaf_uinv,
    leaf_lower,
    leaf_upper,
    sep_rows,
    sep_linv,
    sep_uinv,
    sep_lower,
    sep_upper,
    root_linv,
    root_uinv,
    basis_leaf,
    basis_sep,
    basis_root,
    g_blocks,
    c_blocks,
    block_cols,
):
    ports = b_leaf.shape[1]
    sep_local = b_sep.shape[0]
    root_local = b_root.shape[0]
    sep_width = sep_linv.shape[1]
    selector = (sep_rows[0][:, None] == jnp.arange(sep_width, dtype=jnp.int32)[None, :]).astype(
        jnp.float32
    )
    y_leaf = matmul_exact(leaf_linv, b_leaf)
    contrib = matmul_exact(leaf_lower, y_leaf)
    t_sep = lax.psum_scatter(
        contract_rows(selector, contrib), "inner", scatter_dimension=0, tiled=True
    )
    sep_whole = lax.all_gather(b_sep - t_sep, "inner", axis=0, tiled=True)
    y_sep = matmul_exact(sep_linv, sep_whole)
    t_root = lax.psum_scatter(
        matmul_exact(sep_lower, y_sep), ("outer", "inner"), scatter_dimension=0, tiled=True
    )
    root_rhs = lax.all_gather(b_root - t_root, ("outer", "inner"), axis=0, tiled=True)
    y_root = matmul_exact(root_linv, root_rhs)
    y_root_all = lax.all_gather(y_root, ("outer", "inner"), axis=0, tiled=True)
    x_root = matmul_exact(root_uinv, y_root_all)
    x_root_all = lax.all_gather(x_root, ("outer", "inner"), axis=0, tiled=True)
    z_sep = y_sep - matmul_exact(sep_upper, x_root_all)
    z_sep_all = lax.all_gather(z_sep, "inner", axis=0, tiled=True)
    x_sep = matmul_exact(sep_uinv, z_sep_all)
    x_sep_all = lax.all_gather(x_sep, "inner", axis=0, tiled=True)
    coupled = matmul_exact(selector, x_sep_all)
    x_leaf = matmul_exact(leaf_uinv, y_leaf - matmul_exact(leaf_upper, coupled))
    node_count = float(
        lax.axis_size("outer") * lax.axis_size("inner") * (b_leaf.shape[0] + sep_local + root_local)
    )
    pieces_x = (x_leaf, x_sep, x_root)
    pieces_q = (basis_leaf, basis_sep, basis_root)
    projected = (
        contract_rows(basis_leaf, x_leaf)
        + contract_rows(basis_sep, x_sep)
        + contract_rows(basis_root, x_root)
    )
    coefficients = lax.psum(projected, ("outer", "inner")) / node_count
    cleaned = [
        values - matmul_exact(basis, coefficients) for basis, values in zip(pieces_q, pieces_x)
    ]
    local_gram = (
        contract_rows(cleaned[0], cleaned[0])
        + contract_rows(cleaned[1], cleaned[1])
        + contract_rows(cleaned[2], cleaned[2])
    )
    gram_matrix = lax.psum(local_gram, ("outer", "inner")) / node_count
    chol_lower = jnp.linalg.cholesky(gram_matrix)
    inverse_lower = lax.linalg.triangular_solve(
        chol_lower, jnp.eye(ports, dtype=jnp.float32), left_side=True, lower=True
    )
    v_leaf = matmul_exact(cleaned[0], inverse_lower.T)
    v_sep = matmul_exact(cleaned[1], inverse_lower.T)
    v_root = matmul_exact(cleaned[2], inverse_lower.T)
    block_rows = block_cols.shape[0]
    stored = block_cols.shape[1]
    block_size = g_blocks.shape[1]
    blocked = v_leaf.reshape(block_rows, block_size, ports)
    picked = blocked[block_cols]
    g_tiles = g_blocks.reshape(block_rows, stored, block_size, block_size)
    c_tiles = c_blocks.reshape(block_rows, stored, block_size, block_size)
    g_image = jnp.einsum("rwij,rwjp->rip", g_tiles, picked, precision=lax.Precision.HIGHEST)
    c_image = jnp.einsum("rwij,rwjp->rip", c_tiles, picked, precision=lax.Precision.HIGHEST)
    g_local = jnp.einsum("rip,riq->pq", blocked, g_image, precision=lax.Precision.HIGHEST)
    c_local = jnp.einsum("rip,riq->pq", blocked, c_image, precision=lax.Precision.HIGHEST)
    g_summed, c_summed = lax.psum((g_local, c_local), ("outer", "inner"))
    return (v_leaf, v_sep, v_root, coefficients, g_summed / node_count, c_summed / node_count)


def solution(mesh):
    return jax.shard_map(
        shards,
        mesh=mesh,
        in_specs=(
            P(("outer", "inner"), None),
            P(("outer", "inner"), None),
            P(("outer", "inner"), None),
            P(("outer", "inner"), None),
            P(("outer", "inner"), None),
            P(("outer", "inner"), None),
            P(("outer", "inner"), None),
            P(("outer", "inner"), None),
            P(("outer", "inner"), None),
            P(("outer", "inner"), None),
            P(None, ("outer", "inner")),
            P(("outer", "inner"), None),
            P(("outer", "inner"), None),
            P(("outer", "inner"), None),
            P(("outer", "inner"), None),
            P(("outer", "inner"), None),
            P(("outer", "inner"), None),
            P(("outer", "inner"), None),
            P(("outer", "inner"), None),
            P(("outer", "inner"), None),
        ),
        out_specs=(
            P(("outer", "inner"), None),
            P(("outer", "inner"), None),
            P(("outer", "inner"), None),
            P(),
            P(),
            P(),
        ),
        check_vma=False,
    )
```

profile of v0, /device:TPU:1, one launch (start us, length us, event | category | flops | bytes accessed | tf_op | source)
XLA Modules:
  0.0 1057.3 jit_solution(8577901284034292284)
XLA Ops:
  7.2 1.4 fusion.16
  9.7 1.0 fusion.8
  12.7 112.8 %all-reduce.9.cloned.1.call-done = f32[256,64]{1,0:T(8,128)} async-done(((f32[256,64]{1,0:T(8,128)}), f32[256,64]{1,0:T(8,128)}) %all-reduce.9.cloned.1.call-update) | async-done | bytes 65552
  125.5 0.7 dynamic-slice_subtract_fusion.1
  126.2 25.7 %all_gather.18 = f32[256,64]{1,0:T(8,128)S(1)} all-gather(f32[8,64]{1,0:T(8,128)S(1)} %dynamic-slice_subtract_fusion.1), channel_id=1, replica_groups=mesh['outer'=8,'inner'=32] {'inner'}, dimensions={0}, use_global_device_ids=true | all-gather | bytes 67584 | tf_op jit(solution)/shard_map/all_gather | solution.py:55
  153.3 1.3 copy.47
  155.4 251.8 %all-reduce.11.cloned.1.call-done = f32[2048,64]{1,0:T(8,128)} async-done(((f32[2048,64]{1,0:T(8,128)}), f32[2048,64]{1,0:T(8,128)}) %all-reduce.11.cloned.1.call-update) | async-done | bytes 524304
  407.2 0.7 dynamic-slice_subtract_fusion
  407.9 63.2 %all_gather.19 = f32[2048,64]{1,0:T(8,128)S(1)} all-gather(f32[8,64]{1,0:T(8,128)S(1)} %dynamic-slice_subtract_fusion), channel_id=1, replica_groups=mesh['outer'=8,'inner'=32] {'outer','inner'}, dimensions={0}, use_global_device_ids=true | all-gather | bytes 526336 | tf_op jit(solution)/shard_map/all_gather | solution.py:60
  471.7 60.2 %all_gather.20 = f32[2048,64]{1,0:T(8,128)S(1)} all-gather(f32[8,64]{1,0:T(8,128)S(1)} %convolution_bitcast_fusion.8), channel_id=1, replica_groups=mesh['outer'=8,'inner'=32] {'outer','inner'}, dimensions={0}, use_global_device_ids=true | all-gather | bytes 526336 | tf_op jit(solution)/shard_map/all_gather | solution.py:62
  532.6 60.4 %all_gather.21 = f32[2048,64]{1,0:T(8,128)S(1)} all-gather(f32[8,64]{1,0:T(8,128)S(1)} %bitcast.121), channel_id=1, replica_groups=mesh['outer'=8,'inner'=32] {'outer','inner'}, dimensions={0}, use_global_device_ids=true | all-gather | bytes 526336 | tf_op jit(solution)/shard_map/all_gather | solution.py:64
  593.7 23.3 %all_gather.22 = f32[256,64]{1,0:T(8,128)S(1)} all-gather(f32[8,64]{1,0:T(8,128)S(1)} %fusion.5), channel_id=1, replica_groups=mesh['outer'=8,'inner'=32] {'inner'}, dimensions={0}, use_global_device_ids=true | all-gather | bytes 67584 | tf_op jit(solution)/shard_map/all_gather | solution.py:66
  617.2 23.0 %all_gather.23 = f32[256,64]{1,0:T(8,128)S(1)} all-gather(f32[8,64]{1,0:T(8,128)S(1)} %bitcast.122), channel_id=1, replica_groups=mesh['outer'=8,'inner'=32] {'inner'}, dimensions={0}, use_global_device_ids=true | all-gather | bytes 67584 | tf_op jit(solution)/shard_map/all_gather | solution.py:68
  642.0 1.1 fusion.1
  643.1 237.7 %all-reduce.7.cloned.1.call-done = f32[512,64]{0,1:T(8,128)} async-done(((f32[512,64]{0,1:T(8,128)}), f32[512,64]{0,1:T(8,128)}) %all-reduce.7.cloned.1.call-update) | async-done | bytes 131088 | tf_op jit(solution)/shard_map/psum | solution.py:81
  880.8 0.9 broadcast_multiply_fusion
  883.5 76.0 %psum.29 = f32[64,64]{0,1:T(8,128)S(1)} all-reduce(f32[64,64]{0,1:T(8,128)S(1)} %convolution_add_fusion.1), channel_id=1, replica_groups=mesh['outer'=8,'inner'=32] {'outer','inner'}, use_global_device_ids=true, to_apply=%region_3.0 | all-reduce | flops 4096 | bytes 32768 | tf_op jit(solution)/shard_map/psum | solution.py:90
  959.7 5.8 cholesky.17
  966.9 4.9 custom-call.6
  972.2 0.8 fusion.27
  973.0 0.8 fusion.26
  976.2 73.1 %all-reduce.2 = (f32[64,64]{0,1:T(8,128)S(1)}, f32[64,64]{0,1:T(8,128)S(1)}) all-reduce(f32[64,64]{0,1:T(8,128)S(1)} %convolution_bitcast_fusion.5, f32[64,64]{0,1:T(8,128)S(1)} %convolution_bitcast_fusion.4), channel_id=1, replica_groups=mesh['outer'=8,'inner'=32] {'outer','inner'}, use_global_device_ids=true, to_apply=%region_6.7 | all-reduce | flops 8192 | bytes 65536 | tf_op jit(solution)/shard_map/psum | solution.py:109
  1049.4 0.7 copy.57
  1050.1 0.7 copy.58
  (85 shorter events, 14.6 us)
Async XLA Ops:
  7.2 967.2 %copy-start = (f32[1024,128]{1,0:T(8,128)S(1)}, f32[1024,128]{1,0:T(8,128)}, u32[]{:S(2)}) copy-start(f32[1024,128]{1,0:T(8,128)} %param.38) | copy-start | bytes 1572868
  7.2 1.5 copy-start.6
  7.2 118.3 %all-reduce.9.cloned.1.call-start = ((), (), s32[]{:S(2)}) async-start(), calls=%async_computation.1 | async-start | bytes 262144
  9.0 0.7 copy-start.16
  10.8 396.5 %all-reduce.11.cloned.1.call-start = ((), (), s32[]{:S(2)}) async-start(), calls=%async_computation.2 | async-start | bytes 2097152
  10.8 0.7 copy-start.20
  11.5 114.0 %copy-start.17 = (f32[8,64]{1,0:T(8,128)S(1)}, f32[8,64]{1,0:T(8,128)}, u32[]{:S(2)}) copy-start(f32[8,64]{1,0:T(8,128)} %param.21) | copy-start | bytes 6148
  126.2 25.7 %copy-start.14 = (f32[8,256]{1,0:T(8,128)S(1)}, f32[8,256]{1,0:T(8,128)}, u32[]{:S(2)}) copy-start(f32[8,256]{1,0:T(8,128)} %param.28) | copy-start | bytes 24580
  151.8 0.8 copy-start.8
  154.7 0.7 copy-start.19
  154.7 252.5 %copy-start.18 = (f32[8,64]{1,0:T(8,128)S(1)}, f32[8,64]{1,0:T(8,128)}, u32[]{:S(2)}) copy-start(f32[8,64]{1,0:T(8,128)} %param.22) | copy-start | bytes 6148
  154.7 726.1 %all-reduce.7.cloned.1.call-start = ((), (), s32[]{:S(2)}) async-start(), calls=%async_computation | async-start | bytes 262144 | tf_op jit(solution)/shard_map/psum | solution.py:81
  407.9 63.2 %copy-start.9 = (f32[8,2048]{1,0:T(8,128)S(1)}, f32[8,2048]{1,0:T(8,128)}, u32[]{:S(2)}) copy-start(f32[8,2048]{1,0:T(8,128)} %param.32) | copy-start | bytes 196612
  471.7 60.2 %copy-start.10 = (f32[8,2048]{1,0:T(8,128)S(1)}, f32[8,2048]{1,0:T(8,128)}, u32[]{:S(2)}) copy-start(f32[8,2048]{1,0:T(8,128)} %param.33) | copy-start | bytes 196612
  532.6 60.4 %copy-start.11 = (f32[8,2048]{1,0:T(8,128)S(1)}, f32[8,2048]{1,0:T(8,128)}, u32[]{:S(2)}) copy-start(f32[8,2048]{1,0:T(8,128)} %param.31) | copy-start | bytes 196612
  593.7 23.3 %copy-start.15 = (f32[8,256]{1,0:T(8,128)S(1)}, f32[8,256]{1,0:T(8,128)}, u32[]{:S(2)}) copy-start(f32[8,256]{1,0:T(8,128)} %param.29) | copy-start | bytes 24580
  617.2 23.4 %copy-start.12 = (f32[8,512]{1,0:T(8,128)S(1)}, f32[8,512]{1,0:T(8,128)}, u32[]{:S(2)}) copy-start(f32[8,512]{1,0:T(8,128)} %param.35) | copy-start | bytes 49156
  640.2 0.7 copy-start.13
  640.2 1.0 copy-start.5
  640.6 1.1 copy-start.7
  640.9 1.1 copy-start.1
  881.8 0.8 copy-start.2
  972.2 3.8 copy-start.3
  974.3 1.0 copy-start.4
Sparse Core Ops, SparseCore 0:
  11.8 113.6 all-reduce.8
  154.8 252.3 all-reduce.10
  643.3 237.5 all-reduce.6
where the time goes:
time: 1060 us
  waiting for transfers between devices  602 us (57%)
  blocking collectives  405 us (38%)
  between operations  14.7 us (1%)
  other arithmetic  14.4 us (1%)
  matrix products  14 us (1%)
    unnamed x5, waiting for transfers between devices  365 us
    psum x1, waiting for transfers between devices, shards(): coefficients = lax.psum(projected, ('outer', 'inner')) / node_count  238 us
    psum x1, blocking collectives, shards(): gram_matrix = lax.psum(local_gram, ('outer', 'inner')) / node_count  76 us
    psum x1, blocking collectives, shards(): g_summed, c_summed = lax.psum((g_local, c_local), ('outer', 'inner'))  73.1 us
    all_gather x1, blocking collectives, shards(): lax.all_gather(b_root - t_root, ('outer', 'inner'), axis=0, tiled=True)  63.2 us
    all_gather x1, blocking collectives, shards(): x_root_all = lax.all_gather(x_root, ('outer', 'inner'), axis=0, tiled=True)  60.4 us
    all_gather x1, blocking collectives, shards(): y_root_all = lax.all_gather(y_root, ('outer', 'inner'), axis=0, tiled=True)  60.2 us
    all_gather x1, blocking collectives, shards(): sep_whole = lax.all_gather(b_sep - t_sep, 'inner', axis=0, tiled=True)  25.7 us
  transfers between devices with their start and end apart: 3, of which 3 were waited for; matrix products, arithmetic and copies ran while one was open for 0% of the time, Pallas kernels for 0%

commit v1 on v0

--- a/solution.py
+++ b/solution.py
@@ -78,7 +78,7 @@
         + contract_rows(basis_sep, x_sep)
         + contract_rows(basis_root, x_root)
     )
-    coefficients = lax.psum(projected, ("outer", "inner")) / node_count
+    coefficients = lax.psum(lax.psum(projected, "outer"), "inner") / node_count
     cleaned = [
         values - matmul_exact(basis, coefficients) for basis, values in zip(pieces_q, pieces_x)
     ]

time: 1060 us -> 1000 us (0.943)
  waiting for transfers between devices: 602 us -> 545 us
    psum x1 -> x2, waiting for transfers between devices: 238 us -> 180 us  [shards(): coefficients = lax.psum(lax.psum(projected, 'outer'), 'inner') / node_count]
    unnamed x5 -> x6, waiting for transfers between devices: 365 us -> 365 us
  transfers between devices with their start and end apart: 3 -> 4, of which waited for: 3 -> 4; matrix products, arithmetic and copies ran while one was open for 0% -> 0% of each run, Pallas kernels for 0% -> 0%
where the time goes in v1:
time: 1000 us
  waiting for transfers between devices  545 us (54%)
  blocking collectives  407 us (41%)
  between operations  14.7 us (1%)
  other arithmetic  14.4 us (1%)
  matrix products  14 us (1%)
    unnamed x6, waiting for transfers between devices  365 us
    psum x2, waiting for transfers between devices, shards(): coefficients = lax.psum(lax.psum(projected, 'outer'), 'inner') / node_count  180 us
    psum x1, blocking collectives, shards(): gram_matrix = lax.psum(local_gram, ('outer', 'inner')) / node_count  76.9 us
    psum x1, blocking collectives, shards(): g_summed, c_summed = lax.psum((g_local, c_local), ('outer', 'inner'))  74 us
    all_gather x1, blocking collectives, shards(): lax.all_gather(b_root - t_root, ('outer', 'inner'), axis=0, tiled=True)  63.2 us
    all_gather x1, blocking collectives, shards(): x_root_all = lax.all_gather(x_root, ('outer', 'inner'), axis=0, tiled=True)  60.4 us
    all_gather x1, blocking collectives, shards(): y_root_all = lax.all_gather(y_root, ('outer', 'inner'), axis=0, tiled=True)  60.2 us
    all_gather x1, blocking collectives, shards(): sep_whole = lax.all_gather(b_sep - t_sep, 'inner', axis=0, tiled=True)  25.7 us
  transfers between devices with their start and end apart: 4, of which 4 were waited for; matrix products, arithmetic and copies ran while one was open for 0% of the time, Pallas kernels for 0%

profile of v1, /device:TPU:1, one launch (start us, length us, event | category | flops | bytes accessed | tf_op | source)
XLA Modules:
  0.0 1001.8 jit_solution(6773892369940657298)
XLA Ops:
  7.2 1.4 fusion.16
  9.7 1.0 fusion.8
  12.7 112.8 %all-reduce.12.cloned.1.call-done = f32[256,64]{1,0:T(8,128)} async-done(((f32[256,64]{1,0:T(8,128)}), f32[256,64]{1,0:T(8,128)}) %all-reduce.12.cloned.1.call-update) | async-done | bytes 65552
  125.5 0.7 dynamic-slice_subtract_fusion.1
  126.2 25.7 %all_gather.18 = f32[256,64]{1,0:T(8,128)S(1)} all-gather(f32[8,64]{1,0:T(8,128)S(1)} %dynamic-slice_subtract_fusion.1), channel_id=1, replica_groups=mesh['outer'=8,'inner'=32] {'inner'}, dimensions={0}, use_global_device_ids=true | all-gather | bytes 67584 | tf_op jit(solution)/shard_map/all_gather | solution.py:55
  153.3 1.3 copy.47
  154.7 252.5 %all-reduce.14.cloned.1.call-done = f32[2048,64]{1,0:T(8,128)} async-done(((f32[2048,64]{1,0:T(8,128)}), f32[2048,64]{1,0:T(8,128)}) %all-reduce.14.cloned.1.call-update) | async-done | bytes 524304
  407.9 63.2 %all_gather.19 = f32[2048,64]{1,0:T(8,128)S(1)} all-gather(f32[8,64]{1,0:T(8,128)S(1)} %dynamic-slice_subtract_fusion), channel_id=1, replica_groups=mesh['outer'=8,'inner'=32] {'outer','inner'}, dimensions={0}, use_global_device_ids=true | all-gather | bytes 526336 | tf_op jit(solution)/shard_map/all_gather | solution.py:60
  471.7 60.2 %all_gather.20 = f32[2048,64]{1,0:T(8,128)S(1)} all-gather(f32[8,64]{1,0:T(8,128)S(1)} %convolution_bitcast_fusion.8), channel_id=1, replica_groups=mesh['outer'=8,'inner'=32] {'outer','inner'}, dimensions={0}, use_global_device_ids=true | all-gather | bytes 526336 | tf_op jit(solution)/shard_map/all_gather | solution.py:62
  532.6 60.4 %all_gather.21 = f32[2048,64]{1,0:T(8,128)S(1)} all-gather(f32[8,64]{1,0:T(8,128)S(1)} %bitcast.121), channel_id=1, replica_groups=mesh['outer'=8,'inner'=32] {'outer','inner'}, dimensions={0}, use_global_device_ids=true | all-gather | bytes 526336 | tf_op jit(solution)/shard_map/all_gather | solution.py:64
  593.7 23.3 %all_gather.22 = f32[256,64]{1,0:T(8,128)S(1)} all-gather(f32[8,64]{1,0:T(8,128)S(1)} %fusion.5), channel_id=1, replica_groups=mesh['outer'=8,'inner'=32] {'inner'}, dimensions={0}, use_global_device_ids=true | all-gather | bytes 67584 | tf_op jit(solution)/shard_map/all_gather | solution.py:66
  617.2 23.0 %all_gather.23 = f32[256,64]{1,0:T(8,128)S(1)} all-gather(f32[8,64]{1,0:T(8,128)S(1)} %bitcast.122), channel_id=1, replica_groups=mesh['outer'=8,'inner'=32] {'inner'}, dimensions={0}, use_global_device_ids=true | all-gather | bytes 67584 | tf_op jit(solution)/shard_map/all_gather | solution.py:68
  642.0 1.1 fusion.1
  643.9 63.0 %all-reduce.8.cloned.1.call-done = f32[512,64]{0,1:T(8,128)} async-done(((f32[512,64]{0,1:T(8,128)}), f32[512,64]{0,1:T(8,128)}) %all-reduce.8.cloned.1.call-update) | async-done | bytes 131088 | tf_op jit(solution)/shard_map/psum | solution.py:81
  706.9 116.7 %all-reduce.10.cloned.1.call-done = f32[512,64]{0,1:T(8,128)} async-done(((f32[512,64]{0,1:T(8,128)}), f32[512,64]{0,1:T(8,128)}) %all-reduce.10.cloned.1.call-update) | async-done | bytes 131088 | tf_op jit(solution)/shard_map/psum | solution.py:81
  823.6 0.9 broadcast_multiply_fusion
  826.3 76.9 %psum.37 = f32[64,64]{0,1:T(8,128)S(1)} all-reduce(f32[64,64]{0,1:T(8,128)S(1)} %convolution_add_fusion.1), channel_id=1, replica_groups=mesh['outer'=8,'inner'=32] {'outer','inner'}, use_global_device_ids=true, to_apply=%region_4.0 | all-reduce | flops 4096 | bytes 32768 | tf_op jit(solution)/shard_map/psum | solution.py:90
  903.3 5.8 cholesky.17
  910.5 4.9 custom-call.6
  915.8 0.8 fusion.27
  916.6 0.8 fusion.26
  919.9 74.0 %all-reduce.2 = (f32[64,64]{0,1:T(8,128)S(1)}, f32[64,64]{0,1:T(8,128)S(1)}) all-reduce(f32[64,64]{0,1:T(8,128)S(1)} %convolution_bitcast_fusion.5, f32[64,64]{0,1:T(8,128)S(1)} %convolution_bitcast_fusion.4), channel_id=1, replica_groups=mesh['outer'=8,'inner'=32] {'outer','inner'}, use_global_device_ids=true, to_apply=%region_7.8 | all-reduce | flops 8192 | bytes 65536 | tf_op jit(solution)/shard_map/psum | solution.py:109
  993.8 0.7 copy.57
  994.5 0.7 copy.58
  (88 shorter events, 15.3 us)
Async XLA Ops:
  7.2 910.8 %copy-start = (f32[1024,128]{1,0:T(8,128)S(1)}, f32[1024,128]{1,0:T(8,128)}, u32[]{:S(2)}) copy-start(f32[1024,128]{1,0:T(8,128)} %param.38) | copy-start | bytes 1572868
  7.2 1.5 copy-start.6
  7.2 118.3 %all-reduce.12.cloned.1.call-start = ((), (), s32[]{:S(2)}) async-start(), calls=%async_computation.2 | async-start | bytes 262144
  9.0 0.7 copy-start.16
  10.8 396.4 %all-reduce.14.cloned.1.call-start = ((), (), s32[]{:S(2)}) async-start(), calls=%async_computation.3 | async-start | bytes 2097152
  10.8 0.7 copy-start.20
  11.5 114.0 %copy-start.17 = (f32[8,64]{1,0:T(8,128)S(1)}, f32[8,64]{1,0:T(8,128)}, u32[]{:S(2)}) copy-start(f32[8,64]{1,0:T(8,128)} %param.21) | copy-start | bytes 6148
  126.2 25.7 %copy-start.14 = (f32[8,256]{1,0:T(8,128)S(1)}, f32[8,256]{1,0:T(8,128)}, u32[]{:S(2)}) copy-start(f32[8,256]{1,0:T(8,128)} %param.28) | copy-start | bytes 24580
  151.8 0.8 copy-start.8
  154.7 252.5 %copy-start.18 = (f32[8,64]{1,0:T(8,128)S(1)}, f32[8,64]{1,0:T(8,128)}, u32[]{:S(2)}) copy-start(f32[8,64]{1,0:T(8,128)} %param.22) | copy-start | bytes 6148
  154.7 552.2 %all-reduce.8.cloned.1.call-start = ((), (), s32[]{:S(2)}) async-start(), calls=%async_computation | async-start | bytes 262144 | tf_op jit(solution)/shard_map/psum | solution.py:81
  407.9 63.2 %copy-start.9 = (f32[8,2048]{1,0:T(8,128)S(1)}, f32[8,2048]{1,0:T(8,128)}, u32[]{:S(2)}) copy-start(f32[8,2048]{1,0:T(8,128)} %param.32) | copy-start | bytes 196612
  471.7 60.2 %copy-start.10 = (f32[8,2048]{1,0:T(8,128)S(1)}, f32[8,2048]{1,0:T(8,128)}, u32[]{:S(2)}) copy-start(f32[8,2048]{1,0:T(8,128)} %param.33) | copy-start | bytes 196612
  532.6 60.4 %copy-start.11 = (f32[8,2048]{1,0:T(8,128)S(1)}, f32[8,2048]{1,0:T(8,128)}, u32[]{:S(2)}) copy-start(f32[8,2048]{1,0:T(8,128)} %param.31) | copy-start | bytes 196612
  593.7 23.3 %copy-start.15 = (f32[8,256]{1,0:T(8,128)S(1)}, f32[8,256]{1,0:T(8,128)}, u32[]{:S(2)}) copy-start(f32[8,256]{1,0:T(8,128)} %param.29) | copy-start | bytes 24580
  617.2 23.4 %copy-start.12 = (f32[8,512]{1,0:T(8,128)S(1)}, f32[8,512]{1,0:T(8,128)}, u32[]{:S(2)}) copy-start(f32[8,512]{1,0:T(8,128)} %param.35) | copy-start | bytes 49156
  640.2 0.7 copy-start.13
  640.2 1.0 copy-start.5
  640.6 1.1 copy-start.7
  640.9 1.1 copy-start.1
  643.1 180.5 %all-reduce.10.cloned.1.call-start = ((), (), s32[]{:S(2)}) async-start(), calls=%async_computation.1 | async-start | bytes 262144 | tf_op jit(solution)/shard_map/psum | solution.py:81
  824.5 0.8 copy-start.2
  915.8 3.8 copy-start.3
  918.0 1.0 copy-start.4
  (1 other events, 0.7 us)
Sparse Core Ops, SparseCore 0:
  11.8 113.6 all-reduce.11
  154.8 252.3 all-reduce.13
  643.2 63.5 all-reduce.7
  710.3 113.2 all-reduce.9
